TPU v7x, 32 devices: a whole 2x2x4 slice. The times are simulated.
32 devices in a mesh: rep: 8 (over y, x, core), shard: 4 (over z).
Axes of the slice: x: 2, y: 2, z: 4, core: 2. Of those that a mesh axis runs over, the one named last changes fastest.
Arguments:
- gradients: bfloat16 [8, 96, 2560], P(None, 'shard')
- momentum: float32 [8, 96, 2560], P(None, 'shard'), may hold values from -60 to 60
Outputs:
- updates: bfloat16 [8, 96, 2560], P(None, 'shard', 'rep')
- new_momentum: float32 [8, 96, 2560], P(None, 'shard')
All inputs are finite; a program needn't handle non-finite values.
Results may differ from a plain program's by a relative error of at most 0.0014.
Values may be sent and summed in bfloat16 or wider, within the bound.
A program may use at most 64 MiB of HBM per device.

v0:
```python
import math
import jax
import jax.numpy as jnp
from jax import lax
from jax.sharding import PartitionSpec as P

E = 96
D = 2560
ITERS = 5
momentum_decay = 0.95
norm_floor = 1e-07
quintic_terms = (3.4445, -4.775, 2.0315)


def broadcast(x, axis, root):
    mine = lax.axis_index(axis) == root
    return lax.psum(jnp.where(mine, x, jnp.zeros_like(x)), axis)


def batched_schulz(effective):
    totals = jnp.sqrt(jnp.sum(effective * effective, axis=(1, 2), keepdims=True))
    iterate = effective / (totals + norm_floor)
    for turn in range(ITERS):
        gram_mat = jnp.einsum("kij,klj->kil", iterate, iterate, precision=lax.Precision.HIGHEST)
        square_mat = jnp.einsum("kij,kjl->kil", gram_mat, gram_mat, precision=lax.Precision.HIGHEST)
        poly_mat = quintic_terms[1] * gram_mat + quintic_terms[2] * square_mat
        iterate = quintic_terms[0] * iterate + jnp.einsum(
            "kij,kjl->kil", poly_mat, iterate, precision=lax.Precision.HIGHEST
        )
    return iterate


def per_device(gradients, momentum):
    update_scale = 0.2 * math.sqrt(max(E, D))
    gradient_values = gradients.astype(jnp.float32)
    new_momentum = momentum_decay * momentum + gradient_values
    effective_rows = gradient_values + momentum_decay * new_momentum
    effective = lax.all_to_all(effective_rows, "shard", split_axis=0, concat_axis=1, tiled=True)
    slot_count = effective.shape[0]
    replicas = lax.axis_size("rep")
    column = lax.axis_index("shard")
    replica = lax.axis_index("rep")
    slot_owners = (column * slot_count + jnp.arange(slot_count, dtype=jnp.int32)) % replicas
    owned = slot_owners == replica

    def compute_update(operand):
        return (update_scale * batched_schulz(operand)).astype(jnp.bfloat16)

    def skip_update(operand):
        return jnp.zeros(operand.shape, jnp.bfloat16)

    local_updates = lax.cond(jnp.any(owned), compute_update, skip_update, effective)
    copies = []
    for slot_index in range(slot_count):
        copies.append(broadcast(local_updates[slot_index], "rep", slot_owners[slot_index]))
    stacked = jnp.stack(copies)
    result_rows = lax.all_to_all(stacked, "shard", split_axis=1, concat_axis=0, tiled=True)
    col_width = result_rows.shape[2] // replicas
    kept_cols = lax.dynamic_slice_in_dim(result_rows, replica * col_width, col_width, 2)
    return (kept_cols, new_momentum)


def solution(mesh):
    in_specs = (P(None, "shard", None), P(None, "shard", None))
    out_specs = (P(None, "shard", "rep"), P(None, "shard", None))
    return jax.shard_map(
        per_device, mesh=mesh, in_specs=in_specs, out_specs=out_specs, check_vma=False
    )
```

profile of v0, /device:TPU:0, one launch (start us, length us, event | category | flops | bytes accessed | tf_op | source)
XLA Modules:
  0.0 180.7 jit_solution(16023603056860702382)
XLA Ops:
  7.2 4.4 %convert_add_fusion = (f32[8,24,2560]{2,1,0:T(8,128)}, f32[8,24,2560]{2,1,0:T(8,128)}) fusion(bf16[8,24,2560]{2,1,0:T(8,128)(2,1)} %param.4, f32[8,24,2560]{2,1,0:T(8,128)} %param.5), kind=kLoop, calls=%fused_computation.22 | loop fusion | flops 2457600 | bytes 6881280 | tf_op jit(solution)/shard_map/add | solution.py:37
  11.5 6.3 %all-to-all-start = ((f32[8,24,2560]{2,1,0:T(8,128)}), f32[8,24,2560]{2,1,0:T(8,128)S(1)}, u32[]{:S(2)}, u32[]{:S(2)}) async-start(f32[8,24,2560]{2,1,0:T(8,128)} %get-tuple-element.20), calls=%async_computation | async-start | bytes 3932160 | tf_op jit(solution)/shard_map/all_to_all | solution.py:38
  17.8 0.6 compare_reduce_fusion
  19.2 0.6 fusion.8
  20.9 42.3 %all-to-all-done = f32[8,24,2560]{2,1,0:T(8,128)S(1)} async-done(((f32[8,24,2560]{2,1,0:T(8,128)}), f32[8,24,2560]{2,1,0:T(8,128)S(1)}, u32[]{:S(2)}, u32[]{:S(2)}) %all-to-all-start) | async-done | bytes 1966112 | tf_op jit(solution)/shard_map/all_to_all | solution.py:38
  63.4 21.7 %conditional.1 = (bf16[96,2560]{1,0:T(8,128)(2,1)S(1)}, bf16[96,2560]{1,0:T(8,128)(2,1)S(1)}) conditional(s32[]{:T(128)} %convert_element_type.10, () %tuple.22, f32[2,4,24,2560]{3,2,1,0:T(8,128)S(1)} %bitcast.50), branch_computations={%region_1.2_spmd, %region_2.4_spmd} | conditional | flops 5776128000 | bytes 37847088 | solution.py:52
  63.4 0.4 multiply_reduce_fusion
  64.1 1.9 %fusion.9 = f32[2,96,96]{2,1,0:T(8,128)S(1)} fusion(f32[2,96,2560]{2,1,0:T(8,128)S(1)} %bitcast_divide_fusion), kind=kOutput, calls=%fused_computation.35 | convolution fusion | flops 566231040 | bytes 2039808 | tf_op jit(solution)/shard_map/cond/branch_1_fun/kij,klj->kil/dot_general | solution.py:24
  66.2 1.9 %convolution_add_fusion.4 = f32[2,96,2560]{2,1,0:T(8,128)S(1)} fusion(f32[2,96,96]{2,1,0:T(8,128)S(1)} %fusion.2, f32[2,96,2560]{2,1,0:T(8,128)S(1)} %bitcast_divide_fusion), kind=kOutput, calls=%fused_computation.5 | convolution fusion | flops 567214080 | bytes 4005888 | tf_op jit(solution)/shard_map/cond/branch_1_fun/kij,kjl->kil/dot_general | solution.py:27
  68.2 1.9 %fusion.10 = f32[2,96,96]{2,1,0:T(8,128)S(1)} fusion(f32[2,96,2560]{2,1,0:T(8,128)S(1)} %convolution_add_fusion.4), kind=kOutput, calls=%fused_computation.36 | convolution fusion | flops 566231040 | bytes 2039808 | tf_op jit(solution)/shard_map/cond/branch_1_fun/kij,klj->kil/dot_general | solution.py:24
  70.3 1.9 %convolution_add_fusion.3 = f32[2,96,2560]{2,1,0:T(8,128)S(1)} fusion(f32[2,96,96]{2,1,0:T(8,128)S(1)} %fusion.3, f32[2,96,2560]{2,1,0:T(8,128)S(1)} %convolution_add_fusion.4), kind=kOutput, calls=%fused_computation.4 | convolution fusion | flops 567214080 | bytes 4005888 | tf_op jit(solution)/shard_map/cond/branch_1_fun/kij,kjl->kil/dot_general | solution.py:27
  72.3 1.9 %fusion.11 = f32[2,96,96]{2,1,0:T(8,128)S(1)} fusion(f32[2,96,2560]{2,1,0:T(8,128)S(1)} %convolution_add_fusion.3), kind=kOutput, calls=%fused_computation.37 | convolution fusion | flops 566231040 | bytes 2039808 | tf_op jit(solution)/shard_map/cond/branch_1_fun/kij,klj->kil/dot_general | solution.py:24
  74.4 1.9 %convolution_add_fusion.2 = f32[2,96,2560]{2,1,0:T(8,128)S(1)} fusion(f32[2,96,96]{2,1,0:T(8,128)S(1)} %fusion.4, f32[2,96,2560]{2,1,0:T(8,128)S(1)} %convolution_add_fusion.3), kind=kOutput, calls=%fused_computation.3 | convolution fusion | flops 567214080 | bytes 4005888 | tf_op jit(solution)/shard_map/cond/branch_1_fun/kij,kjl->kil/dot_general | solution.py:27
  76.4 2.1 %fusion.12 = f32[2,96,96]{2,1,0:T(8,128)S(1)} fusion(f32[2,96,2560]{2,1,0:T(8,128)S(1)} %convolution_add_fusion.2), kind=kOutput, calls=%fused_computation.38 | convolution fusion | flops 566231040 | bytes 2039808 | tf_op jit(solution)/shard_map/cond/branch_1_fun/kij,klj->kil/dot_general | solution.py:24
  78.7 1.9 %convolution_add_fusion.1 = f32[2,96,2560]{2,1,0:T(8,128)S(1)} fusion(f32[2,96,96]{2,1,0:T(8,128)S(1)} %fusion.5, f32[2,96,2560]{2,1,0:T(8,128)S(1)} %convolution_add_fusion.2), kind=kOutput, calls=%fused_computation.2 | convolution fusion | flops 567214080 | bytes 4005888 | tf_op jit(solution)/shard_map/cond/branch_1_fun/kij,kjl->kil/dot_general | solution.py:27
  80.6 1.9 %fusion.13 = f32[2,96,96]{2,1,0:T(8,128)S(1)} fusion(f32[2,96,2560]{2,1,0:T(8,128)S(1)} %convolution_add_fusion.1), kind=kOutput, calls=%fused_computation.39 | convolution fusion | flops 566231040 | bytes 2039808 | tf_op jit(solution)/shard_map/cond/branch_1_fun/kij,klj->kil/dot_general | solution.py:24
  82.8 2.0 %fusion.1 = bf16[2,96,2560]{2,1,0:T(8,128)(2,1)S(1)} fusion(f32[2,96,96]{2,1,0:T(8,128)S(1)} %fusion.6, f32[2,96,2560]{2,1,0:T(8,128)S(1)} %convolution_add_fusion.1), kind=kOutput, calls=%fused_computation.6 | convolution fusion | flops 568197120 | bytes 3022848 | tf_op jit(solution)/shard_map/cond/branch_1_fun/kij,kjl->kil/dot_general | solution.py:27
  85.1 1.1 select_bitcast_fusion
  86.2 55.7 %all-reduce.3.cloned.1.call-done = (bf16[1,96,2560]{2,1,0:T(8,128)(2,1)}, bf16[1,96,2560]{2,1,0:T(8,128)(2,1)}) async-done(((bf16[1,96,2560]{2,1,0:T(8,128)(2,1)}, bf16[1,96,2560]{2,1,0:T(8,128)(2,1)}), (bf16[1,96,2560]{2,1,0:T(8,128)(2,1)}, bf16[1,96,2560]{2,1,0:T(8,128)(2,1)})) %all-reduce.3.cloned.1.call-update) | async-done | bytes 983056 | tf_op jit(solution)/shard_map/psum | solution.py:17
  141.8 1.3 pad_maximum_fusion
  143.1 2.0 %copy.10 = bf16[2,96,2560]{2,0,1:T(2,128)(2,1)} copy(bf16[2,96,2560]{2,1,0:T(8,128)(2,1)S(1)} %pad_maximum_fusion) | data formatting | bytes 1966080 | tf_op jit(solution)/shard_map/stack | solution.py:56
  145.1 4.4 %all-to-all-start.1 = ((bf16[2,96,2560]{2,0,1:T(2,128)(2,1)}), bf16[2,96,2560]{2,0,1:T(2,128)(2,1)S(1)}, u32[]{:S(2)}, u32[]{:S(2)}) async-start(bf16[2,96,2560]{2,0,1:T(2,128)(2,1)} %copy.10), calls=%async_computation.1 | async-start | bytes 1966080 | tf_op jit(solution)/shard_map/all_to_all | solution.py:57
  149.5 23.4 %all-to-all-done.1 = bf16[2,96,2560]{2,0,1:T(2,128)(2,1)S(1)} async-done(((bf16[2,96,2560]{2,0,1:T(2,128)(2,1)}), bf16[2,96,2560]{2,0,1:T(2,128)(2,1)S(1)}, u32[]{:S(2)}, u32[]{:S(2)}) %all-to-all-start.1) | async-done | bytes 983072 | tf_op jit(solution)/shard_map/all_to_all | solution.py:57
  173.1 0.8 constant_dynamic-slice_fusion
  (13 shorter events, 1.8 us)
Async XLA Ops:
  11.5 51.7 %all-to-all-start = ((f32[8,24,2560]{2,1,0:T(8,128)}), f32[8,24,2560]{2,1,0:T(8,128)S(1)}, u32[]{:S(2)}, u32[]{:S(2)}) async-start(f32[8,24,2560]{2,1,0:T(8,128)} %get-tuple-element.20), calls=%async_computation | async-start | bytes 3932160 | tf_op jit(solution)/shard_map/all_to_all | solution.py:38
  17.8 124.0 %all-reduce.3.cloned.1.call-start = ((), (), s32[]{:S(2)}) async-start(), calls=%async_computation.2 | async-start | bytes 1966080 | tf_op jit(solution)/shard_map/psum | solution.py:17
  145.1 27.9 %all-to-all-start.1 = ((bf16[2,96,2560]{2,0,1:T(2,128)(2,1)}), bf16[2,96,2560]{2,0,1:T(2,128)(2,1)S(1)}, u32[]{:S(2)}, u32[]{:S(2)}) async-start(bf16[2,96,2560]{2,0,1:T(2,128)(2,1)} %copy.10), calls=%async_computation.1 | async-start | bytes 1966080 | tf_op jit(solution)/shard_map/all_to_all | solution.py:57
Sparse Core Ops, SparseCore 0:
  86.3 55.4 all-reduce.2
where the time goes:
time: 181 us
  waiting for transfers between devices  121 us (67%)
  matrix products  20.6 us (11%)
  between operations  15.9 us (9%)
  starting transfers between devices  10.8 us (6%)
  other arithmetic  8.01 us (4%)
  local copies, waits for them, and re-layouts  3.64 us (2%)
    psum x1, waiting for transfers between devices, broadcast(): return lax.psum(jnp.where(mine, x, jnp.zeros_like(x)), axis)  55.7 us
    all_to_all x1, waiting for transfers between devices, per_device(): lax.all_to_all(effective_rows, 'shard', split_axis=0, concat_axis=1, tile...  42.3 us
    all_to_all x1, waiting for transfers between devices, per_device(): lax.all_to_all(stacked, 'shard', split_axis=1, concat_axis=0, tiled=True)  23.4 us
    dot_general x5, matrix products, batched_schulz(): jnp.einsum('kij,kjl->kil', poly_mat, iterate, precision=lax.Precision.HIG...  9.76 us
    dot_general x5, matrix products, batched_schulz(): jnp.einsum('kij,klj->kil', iterate, iterate, precision=lax.Precision.HIGH...  9.67 us
    all_to_all x1, starting transfers between devices, per_device(): lax.all_to_all(effective_rows, 'shard', split_axis=0, concat_axis=1, tile...  6.32 us
    all_to_all x1, starting transfers between devices, per_device(): lax.all_to_all(stacked, 'shard', split_axis=1, concat_axis=0, tiled=True)  4.45 us
    add x1, other arithmetic, per_device(): effective_rows = gradient_values + momentum_decay * new_momentum  4.36 us
  transfers between devices with their start and end apart: 3, of which 3 were waited for; matrix products, arithmetic and copies ran while one was open for 1% of the time, Pallas kernels for 0%

commit v1 on v0

--- a/solution.py
+++ b/solution.py
@@ -54,7 +54,19 @@
     for slot_index in range(slot_count):
         copies.append(broadcast(local_updates[slot_index], "rep", slot_owners[slot_index]))
     stacked = jnp.stack(copies)
-    result_rows = lax.all_to_all(stacked, "shard", split_axis=1, concat_axis=0, tiled=True)
+    ways, here = (lax.axis_size("shard"), lax.axis_index("shard"))
+    width = stacked.shape[1] // ways
+    shape = list(stacked.shape)
+    shape[1] = width
+    height = shape[0]
+    shape[0] = height * ways
+    full = jnp.zeros(shape, stacked.dtype)
+    for mask in range(ways):
+        part = lax.dynamic_slice_in_dim(stacked, (here ^ mask) * width, width, axis=1)
+        if mask:
+            part = lax.ppermute(part, "shard", [(d, d ^ mask) for d in range(ways)])
+        full = lax.dynamic_update_slice_in_dim(full, part, (here ^ mask) * height, axis=0)
+    result_rows = full
     col_width = result_rows.shape[2] // replicas
     kept_cols = lax.dynamic_slice_in_dim(result_rows, replica * col_width, col_width, 2)
     return (kept_cols, new_momentum)

time: 181 us -> 174 us (0.961)
  waiting for transfers between devices: 121 us -> 115 us
    all_to_all x1 -> x0, waiting for transfers between devices: 23.4 us -> none  [per_device(): lax.all_to_all(stacked, 'shard', split_axis=1, concat_axis=0, tiled=True)]
    ppermute x0 -> x3, waiting for transfers between devices: none -> 17.3 us  [per_device(): part = lax.ppermute(part, 'shard', [(d, d ^ mask) for d in range(ways)])]
    ppermute x0 -> x3, starting transfers between devices: none -> 4.45 us  [per_device(): part = lax.ppermute(part, 'shard', [(d, d ^ mask) for d in range(ways)])]
    all_to_all x1 -> x0, starting transfers between devices: 4.45 us -> none  [per_device(): lax.all_to_all(stacked, 'shard', split_axis=1, concat_axis=0, tiled=True)]
  transfers between devices with their start and end apart: 3 -> 5, of which waited for: 3 -> 4; matrix products, arithmetic and copies ran while one was open for 1% -> 1% of each run, Pallas kernels for 0% -> 0%
where the time goes in v1:
time: 174 us
  waiting for transfers between devices  115 us (66%)
  matrix products  20.6 us (12%)
  between operations  16 us (9%)
  starting transfers between devices  10.8 us (6%)
  other arithmetic  6.76 us (4%)
  local copies, waits for them, and re-layouts  3.94 us (2%)
    psum x1, waiting for transfers between devices, broadcast(): return lax.psum(jnp.where(mine, x, jnp.zeros_like(x)), axis)  55.6 us
    all_to_all x1, waiting for transfers between devices, per_device(): lax.all_to_all(effective_rows, 'shard', split_axis=0, concat_axis=1, tile...  42.2 us
    ppermute x3, waiting for transfers between devices, per_device(): part = lax.ppermute(part, 'shard', [(d, d ^ mask) for d in range(ways)])  17.3 us
    dot_general x5, matrix products, batched_schulz(): jnp.einsum('kij,kjl->kil', poly_mat, iterate, precision=lax.Precision.HIG...  9.76 us
    dot_general x5, matrix products, batched_schulz(): jnp.einsum('kij,klj->kil', iterate, iterate, precision=lax.Precision.HIGH...  9.67 us
    all_to_all x1, starting transfers between devices, per_device(): lax.all_to_all(effective_rows, 'shard', split_axis=0, concat_axis=1, tile...  6.32 us
    ppermute x3, starting transfers between devices, per_device(): part = lax.ppermute(part, 'shard', [(d, d ^ mask) for d in range(ways)])  4.45 us
    add x1, other arithmetic, per_device(): effective_rows = gradient_values + momentum_decay * new_momentum  4.37 us
  transfers between devices with their start and end apart: 5, of which 4 were waited for; matrix products, arithmetic and copies ran while one was open for 1% of the time, Pallas kernels for 0%

profile of v1, /device:TPU:0, one launch (start us, length us, event | category | flops | bytes accessed | tf_op | source)
XLA Modules:
  0.0 173.6 jit_solution(2564470908109951573)
XLA Ops:
  7.2 4.4 %convert_add_fusion = (f32[8,24,2560]{2,1,0:T(8,128)}, f32[8,24,2560]{2,1,0:T(8,128)}) fusion(bf16[8,24,2560]{2,1,0:T(8,128)(2,1)} %param.4, f32[8,24,2560]{2,1,0:T(8,128)} %param.5), kind=kLoop, calls=%fused_computation.22 | loop fusion | flops 2457600 | bytes 6881280 | tf_op jit(solution)/shard_map/add | solution.py:37
  11.5 6.3 %all-to-all-start = ((f32[8,24,2560]{2,1,0:T(8,128)}), f32[8,24,2560]{2,1,0:T(8,128)S(1)}, u32[]{:S(2)}, u32[]{:S(2)}) async-start(f32[8,24,2560]{2,1,0:T(8,128)} %get-tuple-element.20), calls=%async_computation | async-start | bytes 3932160 | tf_op jit(solution)/shard_map/all_to_all | solution.py:38
  21.0 42.2 %all-to-all-done = f32[8,24,2560]{2,1,0:T(8,128)S(1)} async-done(((f32[8,24,2560]{2,1,0:T(8,128)}), f32[8,24,2560]{2,1,0:T(8,128)S(1)}, u32[]{:S(2)}, u32[]{:S(2)}) %all-to-all-start) | async-done | bytes 1966112 | tf_op jit(solution)/shard_map/all_to_all | solution.py:38
  63.4 21.7 %conditional.1 = (bf16[96,2560]{1,0:T(8,128)(2,1)S(1)}, bf16[96,2560]{1,0:T(8,128)(2,1)S(1)}) conditional(s32[]{:T(128)} %convert_element_type.10, () %tuple.22, f32[2,4,24,2560]{3,2,1,0:T(8,128)S(1)} %bitcast.46), branch_computations={%region_1.2_spmd, %region_2.4_spmd} | conditional | flops 5776128000 | bytes 37847088 | solution.py:52
  64.1 1.9 %fusion.9 = f32[2,96,96]{2,1,0:T(8,128)S(1)} fusion(f32[2,96,2560]{2,1,0:T(8,128)S(1)} %bitcast_divide_fusion), kind=kOutput, calls=%fused_computation.43 | convolution fusion | flops 566231040 | bytes 2039808 | tf_op jit(solution)/shard_map/cond/branch_1_fun/kij,klj->kil/dot_general | solution.py:24
  66.2 1.9 %convolution_add_fusion.4 = f32[2,96,2560]{2,1,0:T(8,128)S(1)} fusion(f32[2,96,96]{2,1,0:T(8,128)S(1)} %fusion.2, f32[2,96,2560]{2,1,0:T(8,128)S(1)} %bitcast_divide_fusion), kind=kOutput, calls=%fused_computation.5 | convolution fusion | flops 567214080 | bytes 4005888 | tf_op jit(solution)/shard_map/cond/branch_1_fun/kij,kjl->kil/dot_general | solution.py:27
  68.2 1.9 %fusion.10 = f32[2,96,96]{2,1,0:T(8,128)S(1)} fusion(f32[2,96,2560]{2,1,0:T(8,128)S(1)} %convolution_add_fusion.4), kind=kOutput, calls=%fused_computation.44 | convolution fusion | flops 566231040 | bytes 2039808 | tf_op jit(solution)/shard_map/cond/branch_1_fun/kij,klj->kil/dot_general | solution.py:24
  70.3 1.9 %convolution_add_fusion.3 = f32[2,96,2560]{2,1,0:T(8,128)S(1)} fusion(f32[2,96,96]{2,1,0:T(8,128)S(1)} %fusion.3, f32[2,96,2560]{2,1,0:T(8,128)S(1)} %convolution_add_fusion.4), kind=kOutput, calls=%fused_computation.4 | convolution fusion | flops 567214080 | bytes 4005888 | tf_op jit(solution)/shard_map/cond/branch_1_fun/kij,kjl->kil/dot_general | solution.py:27
  72.3 1.9 %fusion.11 = f32[2,96,96]{2,1,0:T(8,128)S(1)} fusion(f32[2,96,2560]{2,1,0:T(8,128)S(1)} %convolution_add_fusion.3), kind=kOutput, calls=%fused_computation.45 | convolution fusion | flops 566231040 | bytes 2039808 | tf_op jit(solution)/shard_map/cond/branch_1_fun/kij,klj->kil/dot_general | solution.py:24
  74.4 1.9 %convolution_add_fusion.2 = f32[2,96,2560]{2,1,0:T(8,128)S(1)} fusion(f32[2,96,96]{2,1,0:T(8,128)S(1)} %fusion.4, f32[2,96,2560]{2,1,0:T(8,128)S(1)} %convolution_add_fusion.3), kind=kOutput, calls=%fused_computation.3 | convolution fusion | flops 567214080 | bytes 4005888 | tf_op jit(solution)/shard_map/cond/branch_1_fun/kij,kjl->kil/dot_general | solution.py:27
  76.4 2.1 %fusion.12 = f32[2,96,96]{2,1,0:T(8,128)S(1)} fusion(f32[2,96,2560]{2,1,0:T(8,128)S(1)} %convolution_add_fusion.2), kind=kOutput, calls=%fused_computation.46 | convolution fusion | flops 566231040 | bytes 2039808 | tf_op jit(solution)/shard_map/cond/branch_1_fun/kij,klj->kil/dot_general | solution.py:24
  78.7 1.9 %convolution_add_fusion.1 = f32[2,96,2560]{2,1,0:T(8,128)S(1)} fusion(f32[2,96,96]{2,1,0:T(8,128)S(1)} %fusion.5, f32[2,96,2560]{2,1,0:T(8,128)S(1)} %convolution_add_fusion.2), kind=kOutput, calls=%fused_computation.2 | convolution fusion | flops 567214080 | bytes 4005888 | tf_op jit(solution)/shard_map/cond/branch_1_fun/kij,kjl->kil/dot_general | solution.py:27
  80.7 1.9 %fusion.13 = f32[2,96,96]{2,1,0:T(8,128)S(1)} fusion(f32[2,96,2560]{2,1,0:T(8,128)S(1)} %convolution_add_fusion.1), kind=kOutput, calls=%fused_computation.47 | convolution fusion | flops 566231040 | bytes 2039808 | tf_op jit(solution)/shard_map/cond/branch_1_fun/kij,klj->kil/dot_general | solution.py:24
  82.8 2.0 %fusion.1 = bf16[2,96,2560]{2,1,0:T(8,128)(2,1)S(1)} fusion(f32[2,96,96]{2,1,0:T(8,128)S(1)} %fusion.6, f32[2,96,2560]{2,1,0:T(8,128)S(1)} %convolution_add_fusion.1), kind=kOutput, calls=%fused_computation.6 | convolution fusion | flops 568197120 | bytes 3022848 | tf_op jit(solution)/shard_map/cond/branch_1_fun/kij,kjl->kil/dot_general | solution.py:27
  85.1 1.1 select_bitcast_fusion
  86.2 55.6 %all-reduce.3.cloned.1.call-done = (bf16[1,96,2560]{2,1,0:T(8,128)(2,1)}, bf16[1,96,2560]{2,1,0:T(8,128)(2,1)}) async-done(((bf16[1,96,2560]{2,1,0:T(8,128)(2,1)}, bf16[1,96,2560]{2,1,0:T(8,128)(2,1)}), (bf16[1,96,2560]{2,1,0:T(8,128)(2,1)}, bf16[1,96,2560]{2,1,0:T(8,128)(2,1)})) %all-reduce.3.cloned.1.call-update) | async-done | bytes 983056 | tf_op jit(solution)/shard_map/psum | solution.py:17
  141.9 1.1 constant_dynamic-update-slice_fusion.1
  142.9 1.1 constant_dynamic-update-slice_fusion
  144.2 1.4 collective-permute-start
  145.6 2.4 %collective-permute-start.1 = (bf16[2,24,2560]{2,1,0:T(8,128)(2,1)S(1)}, bf16[2,24,2560]{2,1,0:T(8,128)(2,1)S(1)}, u32[]{:S(2)}, u32[]{:S(2)}) collective-permute-start(bf16[2,24,2560]{2,1,0:T(8,128)(2,1)S(1)} %get-tuple-element.25), channel_id=1, source_target_pairs={{0,2},{1,3},{2,0},{3,1},{4,6},{5,7},{6,4},{7,5},{8,10},{9,11},{10,... | collective-permute-start | bytes 737288 | tf_op jit(solution)/shard_map/ppermute | solution.py:67
  148.0 0.6 collective-permute-start.2
  148.6 6.2 %collective-permute-done = bf16[2,24,2560]{2,1,0:T(8,128)(2,1)S(1)} collective-permute-done((bf16[2,24,2560]{2,1,0:T(8,128)(2,1)S(1)}, bf16[2,24,2560]{2,1,0:T(8,128)(2,1)S(1)}, u32[]{:S(2)}, u32[]{:S(2)}) %collective-permute-start) | collective-permute-done | bytes 245792 | tf_op jit(solution)/shard_map/ppermute | solution.py:67
  154.9 11.0 %collective-permute-done.1 = bf16[2,24,2560]{2,1,0:T(8,128)(2,1)S(1)} collective-permute-done((bf16[2,24,2560]{2,1,0:T(8,128)(2,1)S(1)}, bf16[2,24,2560]{2,1,0:T(8,128)(2,1)S(1)}, u32[]{:S(2)}, u32[]{:S(2)}) %collective-permute-start.1) | collective-permute-done | bytes 245792 | tf_op jit(solution)/shard_map/ppermute | solution.py:67
  166.0 0.8 constant_dynamic-slice_fusion.3
  (21 shorter events, 3.5 us)
Async XLA Ops:
  11.5 51.7 %all-to-all-start = ((f32[8,24,2560]{2,1,0:T(8,128)}), f32[8,24,2560]{2,1,0:T(8,128)S(1)}, u32[]{:S(2)}, u32[]{:S(2)}) async-start(f32[8,24,2560]{2,1,0:T(8,128)} %get-tuple-element.20), calls=%async_computation | async-start | bytes 3932160 | tf_op jit(solution)/shard_map/all_to_all | solution.py:38
  17.9 124.0 %all-reduce.3.cloned.1.call-start = ((), (), s32[]{:S(2)}) async-start(), calls=%async_computation.1 | async-start | bytes 1966080 | tf_op jit(solution)/shard_map/psum | solution.py:17
  144.2 10.7 %collective-permute-start = (bf16[2,24,2560]{2,1,0:T(8,128)(2,1)S(1)}, bf16[2,24,2560]{2,1,0:T(8,128)(2,1)S(1)}, u32[]{:S(2)}, u32[]{:S(2)}) collective-permute-start(bf16[2,24,2560]{2,1,0:T(8,128)(2,1)S(1)} %get-tuple-element.26), channel_id=1, source_target_pairs={{0,1},{1,0},{2,3},{3,2},{4,5},{5,4},{6,7},{7,6},{8,9},{9,8},{10,11... | collective-permute-start | bytes 737288 | tf_op jit(solution)/shard_map/ppermute | solution.py:67
  145.6 20.3 %collective-permute-start.1 = (bf16[2,24,2560]{2,1,0:T(8,128)(2,1)S(1)}, bf16[2,24,2560]{2,1,0:T(8,128)(2,1)S(1)}, u32[]{:S(2)}, u32[]{:S(2)}) collective-permute-start(bf16[2,24,2560]{2,1,0:T(8,128)(2,1)S(1)} %get-tuple-element.25), channel_id=1, source_target_pairs={{0,2},{1,3},{2,0},{3,1},{4,6},{5,7},{6,4},{7,5},{8,10},{9,11},{10,... | collective-permute-start | bytes 737288 | tf_op jit(solution)/shard_map/ppermute | solution.py:67
  148.0 17.9 %collective-permute-start.2 = (bf16[2,24,2560]{2,1,0:T(8,128)(2,1)S(1)}, bf16[2,24,2560]{2,1,0:T(8,128)(2,1)S(1)}, u32[]{:S(2)}, u32[]{:S(2)}) collective-permute-start(bf16[2,24,2560]{2,1,0:T(8,128)(2,1)S(1)} %get-tuple-element.24), channel_id=1, source_target_pairs={{0,3},{1,2},{2,1},{3,0},{4,7},{5,6},{6,5},{7,4},{8,11},{9,10},{10,... | collective-permute-start | bytes 737288 | tf_op jit(solution)/shard_map/ppermute | solution.py:67
Sparse Core Ops, SparseCore 0:
  86.3 55.4 all-reduce.2
